TPU v7x, 256 devices: a whole 4x4x8 slice. The times are simulated.
256 devices in a mesh: seq: 16 (over z, x_lo), head: 16 (over x_hi, y, core).
Axes of the slice: x: 4 (x_hi: 2, x_lo: 2; x = x_hi * 2 + x_lo), y: 4, z: 8, core: 2. Of those that a mesh axis runs over, the one named last changes fastest.
Arguments:
- teacher: bfloat16 [3, 4096, 8192], P(None, 'seq', 'head'), may hold values from -10 to 10
- student: bfloat16 [3, 4096, 4096], P(None, 'seq', 'head'), may hold values from -10 to 10
- weights: float32 [4096], P('seq'), may hold values from 64 to 512
- lengths: int32 [4], replicated, may hold values from 1 to 3072, 4096 in all
Outputs:
- row_loss: float32 [4096], P('seq')
- student_grad: float32 [3, 4096, 4096], P(None, 'seq', 'head')
Inputs may be any that keep to these rules, and one draw needn't show every extreme that they name: The lengths sum to 4096; the longest document has exactly 3072 tokens.
All inputs are finite; a program needn't handle non-finite values.
Results may differ from a plain program's by a relative error of at most 0.0044.
Values may be sent and summed in bfloat16 or wider, within the bound.
No kernel may reach another device: no remote copies, remote signals or barrier semaphores. Data moves between devices by JAX's collectives and lax.ppermute only.
A program may use at most 128 MiB of HBM per device.

v0:
```python
import functools
import math

import jax
import jax.numpy as jnp
from jax import lax
from jax.experimental import pallas as pl
from jax.experimental.pallas import tpu as pltpu
from jax.sharding import PartitionSpec as P

AXES = ("seq", "head")
PLANES = (0, 1, 2, 4, 5, 6)
ROUNDS = ((0, 1, 2, 3), (3, 2, 1, 0), (1, 3, 0, 2), (1, 3, 0, 2), (0, 2, 1, 3), (3, 1, 2, 0))
BLOCK = 256
WIDE = 512
NARROW = 256
LOG2E = math.log2(math.e)
LN2 = math.log(2.0)
TEACHER_SCALE = 1.0 / math.sqrt(WIDE)
STUDENT_SCALE = 1.0 / math.sqrt(NARROW)
NEG_FILL = -1e30
SUM_LIMIT = 1e30
LSE_LIMIT = 60.0
MIB = 1 << 20


def place(z, x, g, c):
    return (z * 2 + x) * 16 + g * 2 + c


DEVICES = [(z, x, g, c) for z in range(8) for x in range(2) for g in range(8) for c in range(2)]


def relation_sent(k, quarter, core):
    for r in range(3):
        if ROUNDS[core * 3 + r][k] == quarter:
            return r
    return None


def out_pairs(k):
    pairs = []
    for z, x, g, c in DEVICES:
        r = relation_sent(k, z // 2, c)
        if r is not None:
            pairs.append((place(z, x, g, c), place(PLANES[c * 3 + r], x, g, z % 2)))
    return pairs


def lookup(table, index):
    code = sum(int(value) << (2 * i) for i, value in enumerate(table))
    return lax.shift_right_logical(jnp.int32(code), (2 * index).astype(jnp.int32)) & 3


def back_pairs(k):
    return [(b, a) for a, b in out_pairs(k)]


def swap_pairs(dx, dc):
    return [(place(z, x, g, c), place(z, x ^ dx, g, c ^ dc)) for z, x, g, c in DEVICES if z in PLANES]


def permute(value, pairs):
    return lax.ppermute(value, AXES, pairs)


NT = (((1,), (1,)), ((), ()))
NN = (((1,), (0,)), ((), ()))


def dot(a, b, dims):
    return lax.dot_general(a, b, dims, preferred_element_type=jnp.float32)


def scores(rows, keys):
    t = dot(rows[:, :WIDE], keys[:, :WIDE], NT) * (TEACHER_SCALE * LOG2E)
    s = dot(rows[:, WIDE:], keys[:, WIDE:], NT) * (STUDENT_SCALE * LOG2E)
    return t, s


class Documents:
    def __init__(self, lengths_ref):
        self.starts, self.ends = [], []
        end = jnp.int32(0)
        for d in range(4):
            self.starts.append(end)
            end = end + lengths_ref[d]
            self.ends.append(end)
        self.long_start, self.long_end = self.starts[0], self.ends[0]
        for d in range(1, 4):
            longer = self.ends[d] - self.starts[d] > self.long_end - self.long_start
            self.long_start = jnp.where(longer, self.starts[d], self.long_start)
            self.long_end = jnp.where(longer, self.ends[d], self.long_end)
        self.long_block = jnp.minimum(self.long_start // BLOCK, 16 - LONG_TILES)

    def of(self, positions):
        total = jnp.zeros(positions.shape, jnp.int32)
        for end in self.ends:
            total += jnp.where(positions >= end, 1, 0)
        return total

    def in_longest(self, positions):
        return jnp.logical_and(positions >= self.long_start, positions < self.long_end)

    def of_rows(self, block):
        first = block * BLOCK
        last = first + (BLOCK - 1)
        low, high = jnp.int32(0), jnp.int32(16 * BLOCK)
        for start, end in zip(self.starts, self.ends):
            low = jnp.maximum(low, jnp.where(start <= first, start, 0))
            high = jnp.minimum(high, jnp.where(end > last, end, 16 * BLOCK))
        has_long = jnp.logical_and(last >= self.long_start, first < self.long_end)
        short_low = jnp.where(low == self.long_start, self.long_end, low)
        short_high = jnp.where(high == self.long_end, self.long_start, high)
        has_short = short_high > short_low
        short_block = jnp.minimum(short_low // BLOCK, 16 - SHORT_TILES)
        block_low = low // BLOCK
        return has_long, has_short, short_block, block_low, (high + BLOCK - 1) // BLOCK - block_low


def down(base):
    return base + lax.broadcasted_iota(jnp.int32, (BLOCK, 1), 0)


def across(base):
    return base + lax.broadcasted_iota(jnp.int32, (1, BLOCK), 1)


def fold(v):
    return jnp.sum(v.reshape(BLOCK // 8, 8, BLOCK), axis=0)


def as_row(v):
    return jnp.sum(v, axis=0, keepdims=True)


def as_column(row):
    return jnp.broadcast_to(row, (128, BLOCK)).T


def both_halves(v):
    return jnp.concatenate([v, v], axis=1)


def block_at(ref, index):
    return ref.at[pl.ds(pl.multiple_of(index * BLOCK, BLOCK), BLOCK)]


LONG_TILES = 13
SHORT_TILES = 5
LONG_HALF = 7
SHORT_HALF = 3


def half_block(index, half):
    return (index // 2) * 4 + 2 * half + index % 2


def half_window(first, half, count):
    inside = jnp.bitwise_and(first // 2, 1) == half
    low = jnp.where(inside, first % 2, jnp.where(half == 1, 0, 2))
    return jnp.minimum((first // 4) * 2 + low, 8 - count)


def add_half(docs, own_block, half, own, key_at, sums):
    row_positions = across(own_block * BLOCK)
    has_long, has_short, short_block, _, _ = docs.of_rows(own_block)

    def tiles(first, count, keep_of):
        part_t = jnp.zeros((8, BLOCK), jnp.float32)
        part_c = jnp.zeros((8, BLOCK), jnp.float32)
        part_s = jnp.zeros((8, BLOCK), jnp.float32)
        for j in range(count):
            t, s = scores(key_at(first + j)[...], own[...])
            et = jnp.exp2(t)
            es = jnp.exp2(s)
            keep = keep_of(j, down(half_block(first + j, half) * BLOCK))
            if keep is not None:
                et = jnp.where(keep, et, 0.0)
                es = jnp.where(keep, es, 0.0)
            part_t += fold(et)
            part_s += fold(es)
            part_c += fold(et * (t - s))
        return as_row(part_t), as_row(part_s), as_row(part_c)

    def add(parts, rows):
        for i, part in enumerate(parts):
            sums[i : i + 1] += jnp.where(rows, part, 0.0)

    @pl.when(has_long)
    def _():
        first = half_window(docs.long_start // BLOCK, half, LONG_HALF)

        def keep_of(j, positions):
            return None if 0 < j < LONG_HALF - 1 else docs.in_longest(positions)

        add(tiles(first, LONG_HALF, keep_of), docs.in_longest(row_positions))

    @pl.when(has_short)
    def _():
        first = half_window(short_block, half, SHORT_HALF)
        row_docs = docs.of(row_positions)

        def keep_of(j, positions):
            return docs.of(positions) == row_docs

        add(tiles(first, SHORT_HALF, keep_of), jnp.logical_not(docs.in_longest(row_positions)))


def early_kernel(lengths_ref, blocks_ref, *refs):
    own_refs, side_refs, out_ref, half_ref, sums = refs[:4], refs[4:8], refs[8], refs[9], refs[10]
    docs = Documents(lengths_ref)
    half = jnp.bitwise_and(blocks_ref[0] // 2, 1)
    out_ref[...] = jnp.zeros_like(out_ref)
    for k in range(4):
        index = (blocks_ref[k] // 4) * 2 + blocks_ref[k] % 2
        block_at(half_ref, index)[...] = own_refs[k][:BLOCK]
        block_at(half_ref, jnp.bitwise_xor(index, 1))[...] = side_refs[k][...]
        tail = own_refs[k][BLOCK:].astype(jnp.float32)
        out_ref[k, 3:4] = tail[:1, :BLOCK] + tail[:1, BLOCK : 2 * BLOCK] + tail[:1, 2 * BLOCK :]

    @pl.loop(0, 4)
    def _(rb):
        own_block = blocks_ref[rb]
        sums[...] = jnp.zeros_like(sums)
        own = block_at(half_ref, (own_block // 4) * 2 + own_block % 2)
        add_half(docs, own_block, half, own, functools.partial(block_at, half_ref), sums)
        out_ref[rb, 0:3] = sums[0:3]


def stats_kernel(lengths_ref, blocks_ref, part_ref, half_ref, core_ref, far_ref, *refs):
    out_ref, loss_ref, keys_ref, sums, max_t, max_s = refs
    docs = Documents(lengths_ref)
    half = jnp.bitwise_and(blocks_ref[0] // 2, 1)
    other = 1 - half
    out_ref[...] = jnp.zeros_like(out_ref)
    for i in range(8):
        block_at(keys_ref, half_block(i, half))[...] = half_ref[i * BLOCK : (i + 1) * BLOCK]
    for k in range(4):
        block = jnp.bitwise_xor(blocks_ref[k], 2)
        part = slice(k * BLOCK, (k + 1) * BLOCK)
        block_at(keys_ref, block)[...] = core_ref[part]
        block_at(keys_ref, jnp.bitwise_xor(block, 1))[...] = far_ref[part]

    @pl.loop(0, 4)
    def _(rb):
        own_block = blocks_ref[rb]
        own = block_at(keys_ref, own_block)
        row_positions = across(own_block * BLOCK)
        _, _, _, low_block, all_blocks = docs.of_rows(own_block)
        sums[...] = part_ref[rb]

        def key_at(index):
            return block_at(keys_ref, half_block(index, other))

        add_half(docs, own_block, other, own, key_at, sums)

        fine = jnp.logical_and(jnp.max(sums[0:1]) < SUM_LIMIT, jnp.max(sums[1:2]) < SUM_LIMIT)

        @pl.when(jnp.logical_not(fine))
        def _():
            sums[...] = jnp.zeros_like(sums)
            max_t[...] = jnp.full_like(max_t, NEG_FILL)
            max_s[...] = jnp.full_like(max_s, NEG_FILL)
            row_docs = docs.of(row_positions)
            first = low_block

            @pl.loop(0, all_blocks)
            def _(j):
                t, s = scores(block_at(keys_ref, first + j)[...], own[...])
                keep = docs.of(down((first + j) * BLOCK)) == row_docs
                kept_t = jnp.where(keep, t, NEG_FILL)
                kept_s = jnp.where(keep, s, NEG_FILL)
                old_t = max_t[0:1]
                old_s = max_s[0:1]
                new_t = jnp.maximum(old_t, jnp.max(kept_t, axis=0, keepdims=True))
                new_s = jnp.maximum(old_s, jnp.max(kept_s, axis=0, keepdims=True))
                et = jnp.where(keep, jnp.exp2(kept_t - new_t), 0.0)
                es = jnp.where(keep, jnp.exp2(kept_s - new_s), 0.0)
                shrink_t = jnp.exp2(old_t - new_t)
                sums[0:1] = sums[0:1] * shrink_t + as_row(et)
                sums[1:2] = sums[1:2] * jnp.exp2(old_s - new_s) + as_row(es)
                sums[2:3] = sums[2:3] * shrink_t + as_row(et * (t - s))
                max_t[0:1] = new_t
                max_s[0:1] = new_s

        @pl.when(fine)
        def _():
            max_t[...] = jnp.zeros_like(max_t)
            max_s[...] = jnp.zeros_like(max_s)

        lse_t = jnp.log(sums[0:1]) + LN2 * max_t[0:1]
        lse_s = jnp.log(sums[1:2]) + LN2 * max_s[0:1]
        out_ref[rb, 0:1] = lse_t
        out_ref[rb, 1:2] = lse_s
        out_ref[rb, 3:4] = part_ref[rb, 3:4]
        loss_ref[pl.ds(own_block // 4, 1)] = sums[2:3] * LN2 / sums[0:1] - lse_t + lse_s


def grad_kernel(rb, lengths_ref, blocks_ref, stats_ref, keys_ref, out_ref, row_u, acc, sym):
    docs = Documents(lengths_ref)
    own_block = blocks_ref[rb]
    has_long, has_short, short_block, low_block, all_blocks = docs.of_rows(own_block)
    own = block_at(keys_ref, own_block)
    top = stats_ref[0, 0:2]
    for i in range(1, 16):
        top = jnp.maximum(top, stats_ref[i, 0:2])
    calm = jnp.max(top) <= LSE_LIMIT
    acc[...] = jnp.zeros_like(acc)

    def factors(block):
        return stats_ref[block, 3:4] * jnp.exp(-stats_ref[block, 0:2])

    def tiles(first, count, keep_of):
        mine = factors(own_block)
        row_t = both_halves(as_column(mine[0:1]))
        row_s = both_halves(as_column(mine[1:2]))
        for j in range(count):
            key = block_at(keys_ref, first + j)
            t, s = scores(own[...], key[...])
            key_u = factors(first + j)
            symmetric = jnp.exp2(s) * (row_s + key_u[1:2]) - jnp.exp2(t) * (row_t + key_u[0:1])
            keep = keep_of(j)
            if keep is not None:
                symmetric = jnp.where(keep, symmetric, 0.0)
            sym[:, j * BLOCK : (j + 1) * BLOCK] = symmetric.astype(jnp.bfloat16)
        span = pl.ds(pl.multiple_of(first * BLOCK, BLOCK), count * BLOCK)
        return dot(sym[:, : count * BLOCK], keys_ref[span, WIDE:], NN)

    @pl.when(jnp.logical_and(calm, has_long))
    def _():
        first = docs.long_block

        def keep_of(j):
            if 0 < j < LONG_TILES - 1:
                return None
            return docs.in_longest(across((first + j) * BLOCK))

        total = tiles(first, LONG_TILES, keep_of)
        acc[...] = jnp.where(docs.in_longest(down(own_block * BLOCK)), total, 0.0)

    @pl.when(jnp.logical_and(calm, has_short))
    def _():
        first = short_block
        row_docs = docs.of(down(own_block * BLOCK))

        def keep_of(j):
            return row_docs == docs.of(across((first + j) * BLOCK))

        total = tiles(first, SHORT_TILES, keep_of)
        acc[...] = jnp.where(docs.in_longest(down(own_block * BLOCK)), acc[...], total)

    @pl.when(jnp.logical_not(calm))
    def _():
        for i in range(2):
            row_u[i] = as_column(stats_ref[own_block, i : i + 1] * LOG2E)
        row_u[2] = as_column(stats_ref[own_block, 3:4])
        row_docs = docs.of(down(own_block * BLOCK))
        first = low_block

        @pl.loop(0, all_blocks)
        def _(j):
            key = block_at(keys_ref, first + j)
            t, s = scores(own[...], key[...])
            keep = row_docs == docs.of(across((first + j) * BLOCK))
            key_lse = stats_ref[first + j, 0:2] * LOG2E

            def prob(score, lse):
                return jnp.exp2(jnp.where(keep, score - lse, NEG_FILL))

            pull = both_halves(row_u[2]) * (prob(s, both_halves(row_u[1])) - prob(t, both_halves(row_u[0])))
            pull_t = stats_ref[first + j, 3:4] * (prob(s, key_lse[1:2]) - prob(t, key_lse[0:1]))
            acc[...] += dot((pull + pull_t).astype(jnp.bfloat16), key[:, WIDE:], NN)

    out_ref[...] = (acc[...] * STUDENT_SCALE).astype(out_ref.dtype)


VMEM = pl.BlockSpec(memory_space=pltpu.VMEM)
SMEM = pl.BlockSpec(memory_space=pltpu.SMEM)


def run_early(lengths, blocks, pieces):
    return pl.pallas_call(
        early_kernel,
        out_shape=(
            jax.ShapeDtypeStruct((4, 8, BLOCK), jnp.float32),
            jax.ShapeDtypeStruct((8 * BLOCK, WIDE + NARROW), jnp.bfloat16),
        ),
        in_specs=[SMEM, SMEM] + [VMEM] * 8,
        out_specs=(VMEM, VMEM),
        scratch_shapes=[pltpu.VMEM((8, BLOCK), jnp.float32)],
        compiler_params=pltpu.CompilerParams(vmem_limit_bytes=16 * MIB),
        cost_estimate=pl.CostEstimate(flops=3 * 10**9, bytes_accessed=7 * MIB, transcendentals=0),
        name="early",
    )(lengths, blocks, *pieces)


def run_stats(lengths, blocks, part, half, core, far):
    return pl.pallas_call(
        stats_kernel,
        out_shape=(
            jax.ShapeDtypeStruct((4, 8, BLOCK), jnp.float32),
            jax.ShapeDtypeStruct((4, BLOCK), jnp.float32),
            jax.ShapeDtypeStruct((16 * BLOCK, WIDE + NARROW), jnp.bfloat16),
        ),
        in_specs=[SMEM, SMEM] + [VMEM] * 4,
        out_specs=(VMEM, VMEM, VMEM),
        scratch_shapes=[pltpu.VMEM((8, BLOCK), jnp.float32)] * 3,
        compiler_params=pltpu.CompilerParams(vmem_limit_bytes=20 * MIB),
        cost_estimate=pl.CostEstimate(flops=3 * 10**9, bytes_accessed=7 * MIB, transcendentals=0),
        name="stats",
    )(lengths, blocks, part, half, core, far)


def run_grad(rb, lengths, blocks, stats, keys):
    return pl.pallas_call(
        functools.partial(grad_kernel, rb),
        out_shape=jax.ShapeDtypeStruct((BLOCK, NARROW), jnp.bfloat16),
        in_specs=[SMEM, SMEM, VMEM, VMEM],
        out_specs=VMEM,
        scratch_shapes=[
            pltpu.VMEM((3, BLOCK, 128), jnp.float32),
            pltpu.VMEM((BLOCK, NARROW), jnp.float32),
            pltpu.VMEM((BLOCK, LONG_TILES * BLOCK), jnp.bfloat16),
        ],
        compiler_params=pltpu.CompilerParams(vmem_limit_bytes=16 * MIB),
        cost_estimate=pl.CostEstimate(flops=2 * 10**9, bytes_accessed=7 * MIB, transcendentals=0),
        name="grad",
    )(lengths, blocks, stats, keys)


def after(value, *others):
    return lax.optimization_barrier((value,) + others)[0]


def in_thirds(row):
    high = lax.reduce_precision(row, 8, 7)
    middle = lax.reduce_precision(row - high, 8, 7)
    return [part.astype(jnp.bfloat16) for part in (high, middle, row - high - middle)]


def local(teacher, student, weights, lengths):
    seq = lax.axis_index("seq")
    z, x = seq // 2, seq % 2
    head = lax.axis_index("head")
    c = head % 2
    source = (z // 2) * 2 + c

    items = [ROUNDS[PLANES.index(p)] if p in PLANES else (0, 1, 2, 3) for p in range(8)]
    quarters = [lookup([items[p][k] for p in range(8)], z) for k in range(4)]
    mine = 2 * c + x
    blocks = jnp.stack([q * 4 + mine for q in quarters])

    w_tail = jnp.concatenate(in_thirds(weights.reshape(1, BLOCK)), axis=1)
    w_tail = jnp.pad(w_tail, ((0, 15), (0, 0)))

    def message(k):
        sent = [relation_sent(k, q, core) or 0 for q in range(4) for core in range(2)]
        r = lookup(sent, source)
        vectors = [lax.dynamic_index_in_dim(v, r, 0, False) for v in (teacher, student)]
        return jnp.concatenate([jnp.concatenate(vectors, axis=1), w_tail], axis=0)

    own = [permute(message(k), out_pairs(k)) for k in range(4)]
    mine_only = [v[:BLOCK] for v in own]
    side = [permute(v, swap_pairs(1, 0)) for v in mine_only]
    core = permute(after(jnp.concatenate(mine_only, axis=0), side[1]), swap_pairs(0, 1))
    far = permute(jnp.concatenate(side, axis=0), swap_pairs(0, 1))
    part, half = run_early(lengths, blocks, own + side)
    stats, loss, keys = run_stats(lengths, blocks, part, half, core, far)

    both = jnp.stack([stats, permute(stats, swap_pairs(1, 0))])
    four = [both, permute(both, swap_pairs(0, 1))]
    all_stats = jnp.zeros((16, 8, BLOCK), jnp.float32)
    for flip in range(4):
        for k in range(4):
            where = quarters[k] * 4 + (mine ^ flip)
            all_stats = lax.dynamic_update_slice(
                all_stats, four[flip // 2][flip % 2, k : k + 1], (where, 0, 0)
            )
    grads = []
    for step, dh in enumerate((2, 4, 8)):
        loss = after(loss, all_stats if step == 0 else grads[step - 1])
        came = permute(loss, [(place(z, x, g, c), place(z, x, g, c) ^ dh) for z, x, g, c in DEVICES])
        grads.append(run_grad(step, lengths, blocks, all_stats, keys))
        loss = loss + came
        blocks = after(blocks, loss)
    grads.append(run_grad(3, lengths, blocks, all_stats, keys))

    back = []
    for k in range(4):
        tail = jnp.concatenate(in_thirds(lax.dynamic_slice_in_dim(loss, quarters[k], 1, 0)), axis=0)
        tail = jnp.pad(tail, ((0, 13), (0, 0)))
        back.append(permute(jnp.concatenate([grads[k], tail], axis=0), back_pairs(k)))
    total = sum(v[BLOCK : BLOCK + 3].astype(jnp.float32) for v in back)
    total = jnp.sum(total, axis=0, keepdims=True)
    total = total + permute(
        total, [(place(z, x, g, c), place(z, x, g, c) ^ 1) for z, x, g, c in DEVICES]
    )
    row_loss = total.reshape(BLOCK)

    back = jnp.stack([v[:BLOCK] for v in back])
    came = []
    for r in range(3):
        table = [ROUNDS[core * 3 + r].index(q) for q in range(4) for core in range(2)]
        came.append(lax.dynamic_index_in_dim(back, lookup(table, source), 0, False))
    return (row_loss, jnp.stack(came).astype(jnp.float32))


def solution(mesh):
    return jax.shard_map(
        local,
        mesh=mesh,
        in_specs=(P(None, "seq", "head"), P(None, "seq", "head"), P("seq"), P()),
        out_specs=(P("seq"), P(None, "seq", "head")),
        check_vma=False,
    )
```

profile of v0, /device:TPU:1, one launch (start us, length us, event | category | flops | bytes accessed | tf_op | source)
XLA Modules:
  0.0 181.9 jit_solution(8447774674804151316)
XLA Ops:
  0.6 0.0 copy-start.1
  0.7 1.3 dynamic-slice_bitcast_fusion
  2.0 1.1 dynamic-slice_bitcast_fusion.4
  3.1 0.0 copy-done.1
  3.2 0.1 pad_maximum_fusion.2
  3.3 9.8 %collective-permute-start = (bf16[272,768]{1,0:T(8,128)(2,1)S(1)}, bf16[272,768]{1,0:T(8,128)(2,1)S(1)}, u32[]{:S(2)}, u32[]{:S(2)}) collective-permute-start(bf16[272,768]{1,0:T(8,128)(2,1)S(1)} %get-tuple-element.40), channel_id=1, source_target_pairs={{0,0},{1,160},{2,2},{3,162},{4,4},{5,164},{6,6},{7,166},{8,8},{9,1... | collective-permute-start | bytes 1253384 | tf_op jit(solution)/shard_map/ppermute | solution.py:64
  13.1 1.3 collective-permute-start.1
  14.4 2.4 %collective-permute-start.2 = (bf16[272,768]{1,0:T(8,128)(2,1)S(1)}, bf16[272,768]{1,0:T(8,128)(2,1)S(1)}, u32[]{:S(2)}, u32[]{:S(2)}) collective-permute-start(bf16[272,768]{1,0:T(8,128)(2,1)S(1)} %get-tuple-element.39), channel_id=1, source_target_pairs={{0,64},{1,128},{2,66},{3,130},{4,68},{5,132},{6,70},{7,134},{8,72}... | collective-permute-start | bytes 1253384 | tf_op jit(solution)/shard_map/ppermute | solution.py:64
  16.7 1.9 %collective-permute-start.3 = (bf16[272,768]{1,0:T(8,128)(2,1)S(1)}, bf16[272,768]{1,0:T(8,128)(2,1)S(1)}, u32[]{:S(2)}, u32[]{:S(2)}) collective-permute-start(bf16[272,768]{1,0:T(8,128)(2,1)S(1)} %get-tuple-element.37), channel_id=1, source_target_pairs={{0,32},{1,192},{2,34},{3,194},{4,36},{5,196},{6,38},{7,198},{8,40}... | collective-permute-start | bytes 1253384 | tf_op jit(solution)/shard_map/ppermute | solution.py:64
  18.7 8.4 %collective-permute-done.refs_0_ = bf16[272,768]{1,0:T(8,128)(2,1)S(1)} collective-permute-done((bf16[272,768]{1,0:T(8,128)(2,1)S(1)}, bf16[272,768]{1,0:T(8,128)(2,1)S(1)}, u32[]{:S(2)}, u32[]{:S(2)}) %collective-permute-start) | collective-permute-done | bytes 417824 | tf_op jit(solution)/shard_map/ppermute | solution.py:64
  27.1 3.1 %collective-permute-start.4 = (bf16[256,768]{1,0:T(8,128)(2,1)S(1)}, bf16[256,768]{1,0:T(8,128)(2,1)S(1)}, u32[]{:S(2)}, u32[]{:S(2)}) collective-permute-start(bf16[256,768]{1,0:T(8,128)(2,1)S(1)} %slice.112), channel_id=1, source_target_pairs={{0,16},{1,17},{2,18},{3,19},{4,20},{5,21},{6,22},{7,23},{8,24},{9,... | collective-permute-start | bytes 1179656 | tf_op jit(solution)/shard_map/ppermute | solution.py:64
  30.2 4.3 %collective-permute-done.1.refs_1_ = bf16[272,768]{1,0:T(8,128)(2,1)S(1)} collective-permute-done((bf16[272,768]{1,0:T(8,128)(2,1)S(1)}, bf16[272,768]{1,0:T(8,128)(2,1)S(1)}, u32[]{:S(2)}, u32[]{:S(2)}) %collective-permute-start.1) | collective-permute-done | bytes 417824 | tf_op jit(solution)/shard_map/ppermute | solution.py:64
  34.6 3.1 %collective-permute-start.5 = (bf16[256,768]{1,0:T(8,128)(2,1)S(1)}, bf16[256,768]{1,0:T(8,128)(2,1)S(1)}, u32[]{:S(2)}, u32[]{:S(2)}) collective-permute-start(bf16[256,768]{1,0:T(8,128)(2,1)S(1)} %slice.113), channel_id=1, source_target_pairs={{0,16},{1,17},{2,18},{3,19},{4,20},{5,21},{6,22},{7,23},{8,24},{9,... | collective-permute-start | bytes 1179656 | tf_op jit(solution)/shard_map/ppermute | solution.py:64
  37.7 3.4 %collective-permute-done.2.refs_2_ = bf16[272,768]{1,0:T(8,128)(2,1)S(1)} collective-permute-done((bf16[272,768]{1,0:T(8,128)(2,1)S(1)}, bf16[272,768]{1,0:T(8,128)(2,1)S(1)}, u32[]{:S(2)}, u32[]{:S(2)}) %collective-permute-start.2) | collective-permute-done | bytes 417824 | tf_op jit(solution)/shard_map/ppermute | solution.py:64
  41.1 3.1 %collective-permute-start.6 = (bf16[256,768]{1,0:T(8,128)(2,1)S(1)}, bf16[256,768]{1,0:T(8,128)(2,1)S(1)}, u32[]{:S(2)}, u32[]{:S(2)}) collective-permute-start(bf16[256,768]{1,0:T(8,128)(2,1)S(1)} %slice.114), channel_id=1, source_target_pairs={{0,16},{1,17},{2,18},{3,19},{4,20},{5,21},{6,22},{7,23},{8,24},{9,... | collective-permute-start | bytes 1179656 | tf_op jit(solution)/shard_map/ppermute | solution.py:64
  44.2 4.4 %collective-permute-done.3.refs_3_ = bf16[272,768]{1,0:T(8,128)(2,1)S(1)} collective-permute-done((bf16[272,768]{1,0:T(8,128)(2,1)S(1)}, bf16[272,768]{1,0:T(8,128)(2,1)S(1)}, u32[]{:S(2)}, u32[]{:S(2)}) %collective-permute-start.3) | collective-permute-done | bytes 417824 | tf_op jit(solution)/shard_map/ppermute | solution.py:64
  48.6 0.0 copy-start
  48.6 3.2 %collective-permute-start.7 = (bf16[256,768]{1,0:T(8,128)(2,1)S(1)}, bf16[256,768]{1,0:T(8,128)(2,1)S(1)}, u32[]{:S(2)}, u32[]{:S(2)}) collective-permute-start(bf16[256,768]{1,0:T(8,128)(2,1)S(1)} %slice.115), channel_id=1, source_target_pairs={{0,16},{1,17},{2,18},{3,19},{4,20},{5,21},{6,22},{7,23},{8,24},{9,... | collective-permute-start | bytes 1179656 | tf_op jit(solution)/shard_map/ppermute | solution.py:64
  51.8 1.3 pad_maximum_fusion
  53.1 0.0 collective-permute-done.4.refs_4_
  53.1 0.0 collective-permute-done.5.refs_5_
  53.1 1.1 collective-permute-done.6.refs_6_
  54.2 5.8 %collective-permute-done.7.refs_7_ = bf16[256,768]{1,0:T(8,128)(2,1)S(1)} collective-permute-done((bf16[256,768]{1,0:T(8,128)(2,1)S(1)}, bf16[256,768]{1,0:T(8,128)(2,1)S(1)}, u32[]{:S(2)}, u32[]{:S(2)}) %collective-permute-start.7) | collective-permute-done | bytes 393248 | tf_op jit(solution)/shard_map/ppermute | solution.py:64
  59.9 1.3 pad_maximum_fusion.1
  61.2 1.9 %collective-permute-start.9 = (bf16[1024,768]{1,0:T(8,128)(2,1)}, bf16[1024,768]{1,0:T(8,128)(2,1)}, u32[]{:S(2)}, u32[]{:S(2)}) collective-permute-start(bf16[1024,768]{1,0:T(8,128)(2,1)} %pad_maximum_fusion.1), channel_id=1, source_target_pairs={{0,1},{1,0},{2,3},{3,2},{4,5},{5,4},{6,7},{7,6},{8,9},{9,8},{10,11... | collective-permute-start | bytes 4718600 | tf_op jit(solution)/shard_map/ppermute | solution.py:64
  63.2 2.4 %collective-permute-start.8 = (bf16[1024,768]{1,0:T(8,128)(2,1)}, bf16[1024,768]{1,0:T(8,128)(2,1)}, u32[]{:S(2)}, u32[]{:S(2)}) collective-permute-start(bf16[1024,768]{1,0:T(8,128)(2,1)} %pad_maximum_fusion), channel_id=1, source_target_pairs={{0,1},{1,0},{2,3},{3,2},{4,5},{5,4},{6,7},{7,6},{8,9},{9,8},{10,11... | collective-permute-start | bytes 4718600 | tf_op jit(solution)/shard_map/ppermute | solution.py:64
  65.7 0.1 pad_add_fusion.blocks_ref
  65.8 0.0 copy-done
  65.8 6.6 %early.1 = (f32[4,8,256]{2,1,0:T(8,128)S(1)}, bf16[2048,768]{1,0:T(8,128)(2,1)S(1)}) custom-call(s32[4]{0:T(128)S(1)} %copy-done, s32[4]{0:T(128)S(1)} %pad_add_fusion.blocks_ref, bf16[272,768]{1,0:T(8,128)(2,1)S(1)} %collective-permute-done.refs_0_, bf16[272,768]{1,0:T(8,128)(2,1)S(1)} %collective-permute-done.1.refs_1_, ...), custom_call_target="tpu_custom_call" | custom-call | flops 3000000000 | bytes 7340032 | tf_op jit(solution)/shard_map/early/pallas_call | solution.py:383
  72.4 0.0 collective-permute-done.9.far_ref
  72.4 0.0 collective-permute-done.8.core_ref
  72.4 35.7 %stats.1 = (f32[4,8,256]{2,1,0:T(8,128)S(1)}, f32[4,256]{1,0:T(4,128)S(1)}, bf16[4096,768]{1,0:T(8,128)(2,1)S(1)}) custom-call(s32[4]{0:T(128)S(1)} %copy-done, s32[4]{0:T(128)S(1)} %pad_add_fusion.blocks_ref, f32[4,8,256]{2,1,0:T(8,128)S(1)} %get-tuple-element.14.part_ref, bf16[2048,768]{1,0:T(8,128)(2,1)S(1)} %get-tuple-element.15.half_ref, ...), custom_call_target="tpu_custom_call" | custom-call | flops 3000000000 | bytes 7340032 | tf_op jit(solution)/shard_map/stats/pallas_call | solution.py:399
  108.1 1.9 %collective-permute-start.10 = (f32[4,8,256]{2,1,0:T(8,128)S(1)}, f32[4,8,256]{2,1,0:T(8,128)S(1)}, u32[]{:S(2)}, u32[]{:S(2)}) collective-permute-start(f32[4,8,256]{2,1,0:T(8,128)S(1)} %get-tuple-element.17), channel_id=1, source_target_pairs={{0,16},{1,17},{2,18},{3,19},{4,20},{5,21},{6,22},{7,23},{8,24},{9,... | collective-permute-start | bytes 98312 | tf_op jit(solution)/shard_map/ppermute | solution.py:64
  110.1 2.6 %collective-permute-done.10 = f32[4,8,256]{2,1,0:T(8,128)S(1)} collective-permute-done((f32[4,8,256]{2,1,0:T(8,128)S(1)}, f32[4,8,256]{2,1,0:T(8,128)S(1)}, u32[]{:S(2)}, u32[]{:S(2)}) %collective-permute-start.10) | collective-permute-done | bytes 32800 | tf_op jit(solution)/shard_map/ppermute | solution.py:64
  112.8 1.9 %collective-permute-start.11 = (f32[2,4,8,256]{3,2,1,0:T(8,128)S(1)}, f32[2,4,8,256]{3,2,1,0:T(8,128)S(1)}, u32[]{:S(2)}, u32[]{:S(2)}) collective-permute-start(f32[2,4,8,256]{3,2,1,0:T(8,128)S(1)} %pad_maximum_fusion.11), channel_id=1, source_target_pairs={{0,1},{1,0},{2,3},{3,2},{4,5},{5,4},{6,7},{7,6},{8,9},{9,8},{10,11... | collective-permute-start | bytes 196616 | tf_op jit(solution)/shard_map/ppermute | solution.py:64
  114.7 1.2 collective-permute-done.11
  116.0 1.4 collective-permute-start.12
  117.4 8.3 %grad.4 = bf16[256,256]{1,0:T(8,128)(2,1)S(1)} custom-call(s32[4]{0:T(128)S(1)} %copy-done, s32[4]{0:T(128)S(1)} %pad_add_fusion.blocks_ref, f32[16,8,256]{2,1,0:T(8,128)S(1)} %fusion.25.stats_ref, bf16[4096,768]{1,0:T(8,128)(2,1)S(1)} %get-tuple-element.18.keys_ref), custom_call_target="tpu_custom_call" | custom-call | flops 2000000000 | bytes 7340032 | tf_op jit(solution)/shard_map/grad/pallas_call | solution.py:416
  125.7 0.0 collective-permute-done.12
  125.7 2.7 %collective-permute-start.13 = (f32[4,256]{1,0:T(4,128)S(1)}, f32[4,256]{1,0:T(4,128)S(1)}, u32[]{:S(2)}, u32[]{:S(2)}) collective-permute-start(f32[4,256]{1,0:T(4,128)S(1)} %add.226), channel_id=1, source_target_pairs={{0,4},{1,5},{2,6},{3,7},{4,0},{5,1},{6,2},{7,3},{8,12},{9,13},{10,... | collective-permute-start | bytes 12296 | tf_op jit(solution)/shard_map/ppermute | solution.py:64
  128.4 7.9 %grad.5 = bf16[256,256]{1,0:T(8,128)(2,1)S(1)} custom-call(s32[4]{0:T(128)S(1)} %copy-done, s32[4]{0:T(128)S(1)} %pad_add_fusion.blocks_ref, f32[16,8,256]{2,1,0:T(8,128)S(1)} %fusion.25.stats_ref, bf16[4096,768]{1,0:T(8,128)(2,1)S(1)} %get-tuple-element.18.keys_ref), custom_call_target="tpu_custom_call" | custom-call | flops 2000000000 | bytes 7340032 | tf_op jit(solution)/shard_map/grad/pallas_call | solution.py:416
  136.3 0.0 collective-permute-done.13
  136.4 2.8 %collective-permute-start.14 = (f32[4,256]{1,0:T(4,128)S(1)}, f32[4,256]{1,0:T(4,128)S(1)}, u32[]{:S(2)}, u32[]{:S(2)}) collective-permute-start(f32[4,256]{1,0:T(4,128)S(1)} %add.227), channel_id=1, source_target_pairs={{0,8},{1,9},{2,10},{3,11},{4,12},{5,13},{6,14},{7,15},{8,0},{9,1},... | collective-permute-start | bytes 12296 | tf_op jit(solution)/shard_map/ppermute | solution.py:64
  139.2 7.8 %grad.6 = bf16[256,256]{1,0:T(8,128)(2,1)S(1)} custom-call(s32[4]{0:T(128)S(1)} %copy-done, s32[4]{0:T(128)S(1)} %pad_add_fusion.blocks_ref, f32[16,8,256]{2,1,0:T(8,128)S(1)} %fusion.25.stats_ref, bf16[4096,768]{1,0:T(8,128)(2,1)S(1)} %get-tuple-element.18.keys_ref), custom_call_target="tpu_custom_call" | custom-call | flops 2000000000 | bytes 7340032 | tf_op jit(solution)/shard_map/grad/pallas_call | solution.py:416
  147.0 0.0 collective-permute-done.14
  147.1 10.9 %collective-permute-start.15 = (bf16[272,256]{1,0:T(8,128)(2,1)S(1)}, bf16[272,256]{1,0:T(8,128)(2,1)S(1)}, u32[]{:S(2)}, u32[]{:S(2)}) collective-permute-start(bf16[272,256]{1,0:T(8,128)(2,1)S(1)} %pad_maximum_fusion.7), channel_id=1, source_target_pairs={{0,0},{160,1},{2,2},{162,3},{4,4},{164,5},{6,6},{166,7},{8,8},{168... | collective-permute-start | bytes 417800 | tf_op jit(solution)/shard_map/ppermute | solution.py:64
  158.0 1.3 collective-permute-start.16
  159.3 2.0 %collective-permute-start.17 = (bf16[272,256]{1,0:T(8,128)(2,1)S(1)}, bf16[272,256]{1,0:T(8,128)(2,1)S(1)}, u32[]{:S(2)}, u32[]{:S(2)}) collective-permute-start(bf16[272,256]{1,0:T(8,128)(2,1)S(1)} %pad_maximum_fusion.9), channel_id=1, source_target_pairs={{64,0},{128,1},{66,2},{130,3},{68,4},{132,5},{70,6},{134,7},{72,8}... | collective-permute-start | bytes 417800 | tf_op jit(solution)/shard_map/ppermute | solution.py:64
  161.3 8.3 %grad.7 = bf16[256,256]{1,0:T(8,128)(2,1)S(1)} custom-call(s32[4]{0:T(128)S(1)} %copy-done, s32[4]{0:T(128)S(1)} %pad_add_fusion.blocks_ref, f32[16,8,256]{2,1,0:T(8,128)S(1)} %fusion.25.stats_ref, bf16[4096,768]{1,0:T(8,128)(2,1)S(1)} %get-tuple-element.18.keys_ref), custom_call_target="tpu_custom_call" | custom-call | flops 2000000000 | bytes 7340032 | tf_op jit(solution)/shard_map/grad/pallas_call | solution.py:416
  169.6 1.9 %collective-permute-start.18 = (bf16[272,256]{1,0:T(8,128)(2,1)S(1)}, bf16[272,256]{1,0:T(8,128)(2,1)S(1)}, u32[]{:S(2)}, u32[]{:S(2)}) collective-permute-start(bf16[272,256]{1,0:T(8,128)(2,1)S(1)} %pad_maximum_fusion.10), channel_id=1, source_target_pairs={{32,0},{192,1},{34,2},{194,3},{36,4},{196,5},{38,6},{198,7},{40,8}... | collective-permute-start | bytes 417800 | tf_op jit(solution)/shard_map/ppermute | solution.py:64
  171.6 0.0 collective-permute-done.15
  171.6 0.0 collective-permute-done.16
  171.6 0.0 collective-permute-done.17
  171.6 8.5 %collective-permute-done.18 = bf16[272,256]{1,0:T(8,128)(2,1)S(1)} collective-permute-done((bf16[272,256]{1,0:T(8,128)(2,1)S(1)}, bf16[272,256]{1,0:T(8,128)(2,1)S(1)}, u32[]{:S(2)}, u32[]{:S(2)}) %collective-permute-start.18) | collective-permute-done | bytes 139296 | tf_op jit(solution)/shard_map/ppermute | solution.py:64
  180.1 0.1 collective-permute-start.19
  180.3 0.1 pad_maximum_fusion.6
  180.4 0.9 maximum_convert_fusion
  181.4 0.0 collective-permute-done.19
  181.4 0.6 add.236
  (45 shorter events, 0.5 us)
Async XLA Ops:
  0.6 2.5 %copy-start.1 = (f32[256]{0:T(256)S(1)}, f32[256]{0:T(256)}, u32[]{:S(2)}) copy-start(f32[256]{0:T(256)} %param.6) | copy-start | bytes 3076
  3.3 23.7 %collective-permute-start = (bf16[272,768]{1,0:T(8,128)(2,1)S(1)}, bf16[272,768]{1,0:T(8,128)(2,1)S(1)}, u32[]{:S(2)}, u32[]{:S(2)}) collective-permute-start(bf16[272,768]{1,0:T(8,128)(2,1)S(1)} %get-tuple-element.40), channel_id=1, source_target_pairs={{0,0},{1,160},{2,2},{3,162},{4,4},{5,164},{6,6},{7,166},{8,8},{9,1... | collective-permute-start | bytes 1253384 | tf_op jit(solution)/shard_map/ppermute | solution.py:64
  13.1 21.5 %collective-permute-start.1 = (bf16[272,768]{1,0:T(8,128)(2,1)S(1)}, bf16[272,768]{1,0:T(8,128)(2,1)S(1)}, u32[]{:S(2)}, u32[]{:S(2)}) collective-permute-start(bf16[272,768]{1,0:T(8,128)(2,1)S(1)} %get-tuple-element.38), channel_id=1, source_target_pairs={{64,0},{65,192},{66,2},{67,194},{68,4},{69,196},{70,6},{71,198},{7... | collective-permute-start | bytes 1253384 | tf_op jit(solution)/shard_map/ppermute | solution.py:64
  14.4 26.7 %collective-permute-start.2 = (bf16[272,768]{1,0:T(8,128)(2,1)S(1)}, bf16[272,768]{1,0:T(8,128)(2,1)S(1)}, u32[]{:S(2)}, u32[]{:S(2)}) collective-permute-start(bf16[272,768]{1,0:T(8,128)(2,1)S(1)} %get-tuple-element.39), channel_id=1, source_target_pairs={{0,64},{1,128},{2,66},{3,130},{4,68},{5,132},{6,70},{7,134},{8,72}... | collective-permute-start | bytes 1253384 | tf_op jit(solution)/shard_map/ppermute | solution.py:64
  16.7 31.9 %collective-permute-start.3 = (bf16[272,768]{1,0:T(8,128)(2,1)S(1)}, bf16[272,768]{1,0:T(8,128)(2,1)S(1)}, u32[]{:S(2)}, u32[]{:S(2)}) collective-permute-start(bf16[272,768]{1,0:T(8,128)(2,1)S(1)} %get-tuple-element.37), channel_id=1, source_target_pairs={{0,32},{1,192},{2,34},{3,194},{4,36},{5,196},{6,38},{7,198},{8,40}... | collective-permute-start | bytes 1253384 | tf_op jit(solution)/shard_map/ppermute | solution.py:64
  27.1 26.0 %collective-permute-start.4 = (bf16[256,768]{1,0:T(8,128)(2,1)S(1)}, bf16[256,768]{1,0:T(8,128)(2,1)S(1)}, u32[]{:S(2)}, u32[]{:S(2)}) collective-permute-start(bf16[256,768]{1,0:T(8,128)(2,1)S(1)} %slice.112), channel_id=1, source_target_pairs={{0,16},{1,17},{2,18},{3,19},{4,20},{5,21},{6,22},{7,23},{8,24},{9,... | collective-permute-start | bytes 1179656 | tf_op jit(solution)/shard_map/ppermute | solution.py:64
  34.6 18.5 %collective-permute-start.5 = (bf16[256,768]{1,0:T(8,128)(2,1)S(1)}, bf16[256,768]{1,0:T(8,128)(2,1)S(1)}, u32[]{:S(2)}, u32[]{:S(2)}) collective-permute-start(bf16[256,768]{1,0:T(8,128)(2,1)S(1)} %slice.113), channel_id=1, source_target_pairs={{0,16},{1,17},{2,18},{3,19},{4,20},{5,21},{6,22},{7,23},{8,24},{9,... | collective-permute-start | bytes 1179656 | tf_op jit(solution)/shard_map/ppermute | solution.py:64
  41.1 13.1 %collective-permute-start.6 = (bf16[256,768]{1,0:T(8,128)(2,1)S(1)}, bf16[256,768]{1,0:T(8,128)(2,1)S(1)}, u32[]{:S(2)}, u32[]{:S(2)}) collective-permute-start(bf16[256,768]{1,0:T(8,128)(2,1)S(1)} %slice.114), channel_id=1, source_target_pairs={{0,16},{1,17},{2,18},{3,19},{4,20},{5,21},{6,22},{7,23},{8,24},{9,... | collective-permute-start | bytes 1179656 | tf_op jit(solution)/shard_map/ppermute | solution.py:64
  48.6 17.1 %copy-start = (s32[4]{0:T(128)S(1)}, s32[4]{0:T(128)}, u32[]{:S(2)}) copy-start(s32[4]{0:T(128)} %lengths_ref.11) | copy-start | bytes 52
  48.6 11.3 %collective-permute-start.7 = (bf16[256,768]{1,0:T(8,128)(2,1)S(1)}, bf16[256,768]{1,0:T(8,128)(2,1)S(1)}, u32[]{:S(2)}, u32[]{:S(2)}) collective-permute-start(bf16[256,768]{1,0:T(8,128)(2,1)S(1)} %slice.115), channel_id=1, source_target_pairs={{0,16},{1,17},{2,18},{3,19},{4,20},{5,21},{6,22},{7,23},{8,24},{9,... | collective-permute-start | bytes 1179656 | tf_op jit(solution)/shard_map/ppermute | solution.py:64
  61.2 11.1 %collective-permute-start.9 = (bf16[1024,768]{1,0:T(8,128)(2,1)}, bf16[1024,768]{1,0:T(8,128)(2,1)}, u32[]{:S(2)}, u32[]{:S(2)}) collective-permute-start(bf16[1024,768]{1,0:T(8,128)(2,1)} %pad_maximum_fusion.1), channel_id=1, source_target_pairs={{0,1},{1,0},{2,3},{3,2},{4,5},{5,4},{6,7},{7,6},{8,9},{9,8},{10,11... | collective-permute-start | bytes 4718600 | tf_op jit(solution)/shard_map/ppermute | solution.py:64
  63.2 9.2 %collective-permute-start.8 = (bf16[1024,768]{1,0:T(8,128)(2,1)}, bf16[1024,768]{1,0:T(8,128)(2,1)}, u32[]{:S(2)}, u32[]{:S(2)}) collective-permute-start(bf16[1024,768]{1,0:T(8,128)(2,1)} %pad_maximum_fusion), channel_id=1, source_target_pairs={{0,1},{1,0},{2,3},{3,2},{4,5},{5,4},{6,7},{7,6},{8,9},{9,8},{10,11... | collective-permute-start | bytes 4718600 | tf_op jit(solution)/shard_map/ppermute | solution.py:64
  108.1 4.7 %collective-permute-start.10 = (f32[4,8,256]{2,1,0:T(8,128)S(1)}, f32[4,8,256]{2,1,0:T(8,128)S(1)}, u32[]{:S(2)}, u32[]{:S(2)}) collective-permute-start(f32[4,8,256]{2,1,0:T(8,128)S(1)} %get-tuple-element.17), channel_id=1, source_target_pairs={{0,16},{1,17},{2,18},{3,19},{4,20},{5,21},{6,22},{7,23},{8,24},{9,... | collective-permute-start | bytes 98312 | tf_op jit(solution)/shard_map/ppermute | solution.py:64
  112.8 3.1 %collective-permute-start.11 = (f32[2,4,8,256]{3,2,1,0:T(8,128)S(1)}, f32[2,4,8,256]{3,2,1,0:T(8,128)S(1)}, u32[]{:S(2)}, u32[]{:S(2)}) collective-permute-start(f32[2,4,8,256]{3,2,1,0:T(8,128)S(1)} %pad_maximum_fusion.11), channel_id=1, source_target_pairs={{0,1},{1,0},{2,3},{3,2},{4,5},{5,4},{6,7},{7,6},{8,9},{9,8},{10,11... | collective-permute-start | bytes 196616 | tf_op jit(solution)/shard_map/ppermute | solution.py:64
  116.0 9.7 %collective-permute-start.12 = (f32[4,256]{1,0:T(4,128)S(1)}, f32[4,256]{1,0:T(4,128)S(1)}, u32[]{:S(2)}, u32[]{:S(2)}) collective-permute-start(f32[4,256]{1,0:T(4,128)S(1)} %get-tuple-element.20), channel_id=1, source_target_pairs={{0,2},{1,3},{2,0},{3,1},{4,6},{5,7},{6,4},{7,5},{8,10},{9,11},{10,... | collective-permute-start | bytes 12296 | tf_op jit(solution)/shard_map/ppermute | solution.py:64
  125.7 10.6 %collective-permute-start.13 = (f32[4,256]{1,0:T(4,128)S(1)}, f32[4,256]{1,0:T(4,128)S(1)}, u32[]{:S(2)}, u32[]{:S(2)}) collective-permute-start(f32[4,256]{1,0:T(4,128)S(1)} %add.226), channel_id=1, source_target_pairs={{0,4},{1,5},{2,6},{3,7},{4,0},{5,1},{6,2},{7,3},{8,12},{9,13},{10,... | collective-permute-start | bytes 12296 | tf_op jit(solution)/shard_map/ppermute | solution.py:64
  136.4 10.6 %collective-permute-start.14 = (f32[4,256]{1,0:T(4,128)S(1)}, f32[4,256]{1,0:T(4,128)S(1)}, u32[]{:S(2)}, u32[]{:S(2)}) collective-permute-start(f32[4,256]{1,0:T(4,128)S(1)} %add.227), channel_id=1, source_target_pairs={{0,8},{1,9},{2,10},{3,11},{4,12},{5,13},{6,14},{7,15},{8,0},{9,1},... | collective-permute-start | bytes 12296 | tf_op jit(solution)/shard_map/ppermute | solution.py:64
  147.1 24.5 %collective-permute-start.15 = (bf16[272,256]{1,0:T(8,128)(2,1)S(1)}, bf16[272,256]{1,0:T(8,128)(2,1)S(1)}, u32[]{:S(2)}, u32[]{:S(2)}) collective-permute-start(bf16[272,256]{1,0:T(8,128)(2,1)S(1)} %pad_maximum_fusion.7), channel_id=1, source_target_pairs={{0,0},{160,1},{2,2},{162,3},{4,4},{164,5},{6,6},{166,7},{8,8},{168... | collective-permute-start | bytes 417800 | tf_op jit(solution)/shard_map/ppermute | solution.py:64
  158.0 13.6 %collective-permute-start.16 = (bf16[272,256]{1,0:T(8,128)(2,1)S(1)}, bf16[272,256]{1,0:T(8,128)(2,1)S(1)}, u32[]{:S(2)}, u32[]{:S(2)}) collective-permute-start(bf16[272,256]{1,0:T(8,128)(2,1)S(1)} %pad_maximum_fusion.8), channel_id=1, source_target_pairs={{0,64},{192,65},{2,66},{194,67},{4,68},{196,69},{6,70},{198,71},{8... | collective-permute-start | bytes 417800 | tf_op jit(solution)/shard_map/ppermute | solution.py:64
  159.3 12.3 %collective-permute-start.17 = (bf16[272,256]{1,0:T(8,128)(2,1)S(1)}, bf16[272,256]{1,0:T(8,128)(2,1)S(1)}, u32[]{:S(2)}, u32[]{:S(2)}) collective-permute-start(bf16[272,256]{1,0:T(8,128)(2,1)S(1)} %pad_maximum_fusion.9), channel_id=1, source_target_pairs={{64,0},{128,1},{66,2},{130,3},{68,4},{132,5},{70,6},{134,7},{72,8}... | collective-permute-start | bytes 417800 | tf_op jit(solution)/shard_map/ppermute | solution.py:64
  169.6 10.5 %collective-permute-start.18 = (bf16[272,256]{1,0:T(8,128)(2,1)S(1)}, bf16[272,256]{1,0:T(8,128)(2,1)S(1)}, u32[]{:S(2)}, u32[]{:S(2)}) collective-permute-start(bf16[272,256]{1,0:T(8,128)(2,1)S(1)} %pad_maximum_fusion.10), channel_id=1, source_target_pairs={{32,0},{192,1},{34,2},{194,3},{36,4},{196,5},{38,6},{198,7},{40,8}... | collective-permute-start | bytes 417800 | tf_op jit(solution)/shard_map/ppermute | solution.py:64
  180.1 1.2 collective-permute-start.19
where the time goes:
time: 182 us
  Pallas kernels  74.6 us (41%)
  starting transfers between devices  59.1 us (32%)
  waiting for transfers between devices  39.6 us (22%)
  other arithmetic  4.53 us (2%)
  local copies, waits for them, and re-layouts  2.73 us (2%)
    ppermute x20, starting transfers between devices, permute(): return lax.ppermute(value, AXES, pairs)  59.1 us
    ppermute x20, waiting for transfers between devices, permute(): return lax.ppermute(value, AXES, pairs)  39.6 us
    pallas_call x1, Pallas kernels, run_stats(): pl.pallas_call(stats_kernel, out_shape=(jax.ShapeDtypeStruct((4, 8, BLOCK...  35.7 us
    pallas_call x4, Pallas kernels, run_grad(): pl.pallas_call(functools.partial(grad_kernel, rb), out_shape=jax.ShapeDty...  32.3 us
    pallas_call x1, Pallas kernels, run_early(): pl.pallas_call(early_kernel, out_shape=(jax.ShapeDtypeStruct((4, 8, BLOCK...  6.58 us
  transfers between devices with their start and end apart: 20, of which 9 were waited for; matrix products, arithmetic and copies ran while one was open for 1% of the time, Pallas kernels for 21%

commit v1 on v0

--- a/solution.py
+++ b/solution.py
@@ -229,18 +229,24 @@
 
 
 def stats_kernel(lengths_ref, blocks_ref, part_ref, half_ref, core_ref, far_ref, *refs):
-    out_ref, loss_ref, keys_ref, sums, max_t, max_s = refs
+    out_ref, loss_ref, keys_ref, sums, max_t, max_s, arrived = refs
     docs = Documents(lengths_ref)
     half = jnp.bitwise_and(blocks_ref[0] // 2, 1)
     other = 1 - half
     out_ref[...] = jnp.zeros_like(out_ref)
+    copies = []
+    for k in range(4):
+        block = jnp.bitwise_xor(blocks_ref[k], 2)
+        part = pl.ds(k * BLOCK, BLOCK)
+        for i, (source, target) in enumerate(((core_ref, block), (far_ref, jnp.bitwise_xor(block, 1)))):
+            copies.append(
+                pltpu.make_async_copy(source.at[part], block_at(keys_ref, target), arrived.at[2 * k + i])
+            )
+            copies[-1].start()
     for i in range(8):
         block_at(keys_ref, half_block(i, half))[...] = half_ref[i * BLOCK : (i + 1) * BLOCK]
-    for k in range(4):
-        block = jnp.bitwise_xor(blocks_ref[k], 2)
-        part = slice(k * BLOCK, (k + 1) * BLOCK)
-        block_at(keys_ref, block)[...] = core_ref[part]
-        block_at(keys_ref, jnp.bitwise_xor(block, 1))[...] = far_ref[part]
+    for copy in copies:
+        copy.wait()
 
     @pl.loop(0, 4)
     def _(rb):
@@ -377,6 +383,7 @@
 
 VMEM = pl.BlockSpec(memory_space=pltpu.VMEM)
 SMEM = pl.BlockSpec(memory_space=pltpu.SMEM)
+ANY = pl.BlockSpec(memory_space=pl.ANY)
 
 
 def run_early(lengths, blocks, pieces):
@@ -403,9 +410,9 @@
             jax.ShapeDtypeStruct((4, BLOCK), jnp.float32),
             jax.ShapeDtypeStruct((16 * BLOCK, WIDE + NARROW), jnp.bfloat16),
         ),
-        in_specs=[SMEM, SMEM] + [VMEM] * 4,
+        in_specs=[SMEM, SMEM, VMEM, VMEM, ANY, ANY],
         out_specs=(VMEM, VMEM, VMEM),
-        scratch_shapes=[pltpu.VMEM((8, BLOCK), jnp.float32)] * 3,
+        scratch_shapes=[pltpu.VMEM((8, BLOCK), jnp.float32)] * 3 + [pltpu.SemaphoreType.DMA((8,))],
         compiler_params=pltpu.CompilerParams(vmem_limit_bytes=20 * MIB),
         cost_estimate=pl.CostEstimate(flops=3 * 10**9, bytes_accessed=7 * MIB, transcendentals=0),
         name="stats",

time: 182 us -> 180 us (0.989)
  the two profiles are of different devices: /device:TPU:1 before, /device:TPU:2 now
where the time goes in v1:
time: 180 us; the launch traced here: 178 us
  Pallas kernels  74.7 us (42%)
  starting transfers between devices  60 us (33%)
  waiting for transfers between devices  34.5 us (19%)
  other arithmetic  4.53 us (3%)
  local copies, waits for them, and re-layouts  2.73 us (2%)
    ppermute x20, starting transfers between devices, permute(): return lax.ppermute(value, AXES, pairs)  60 us
    pallas_call x1, Pallas kernels, run_stats(): pl.pallas_call(stats_kernel, out_shape=(jax.ShapeDtypeStruct((4, 8, BLOCK...  35.8 us
    ppermute x20, waiting for transfers between devices, permute(): return lax.ppermute(value, AXES, pairs)  34.5 us
    pallas_call x4, Pallas kernels, run_grad(): pl.pallas_call(functools.partial(grad_kernel, rb), out_shape=jax.ShapeDty...  32.3 us
    pallas_call x1, Pallas kernels, run_early(): pl.pallas_call(early_kernel, out_shape=(jax.ShapeDtypeStruct((4, 8, BLOCK...  6.58 us
  transfers between devices with their start and end apart: 20, of which 7 were waited for; matrix products, arithmetic and copies ran while one was open for 2% of the time, Pallas kernels for 22%

profile of v1, /device:TPU:2, one launch (start us, length us, event | category | flops | bytes accessed | tf_op | source)
XLA Modules:
  0.0 177.8 jit_solution(4195362591743602885)
XLA Ops:
  0.6 0.0 copy-start.1
  0.7 1.3 dynamic-slice_bitcast_fusion
  2.0 1.1 dynamic-slice_bitcast_fusion.4
  3.1 0.0 copy-done.1
  3.2 0.1 pad_maximum_fusion.2
  3.3 0.7 collective-permute-start
  4.0 1.3 collective-permute-start.1
  5.3 5.8 %collective-permute-start.2 = (bf16[272,768]{1,0:T(8,128)(2,1)S(1)}, bf16[272,768]{1,0:T(8,128)(2,1)S(1)}, u32[]{:S(2)}, u32[]{:S(2)}) collective-permute-start(bf16[272,768]{1,0:T(8,128)(2,1)S(1)} %get-tuple-element.39), channel_id=1, source_target_pairs={{0,64},{1,128},{2,66},{3,130},{4,68},{5,132},{6,70},{7,134},{8,72}... | collective-permute-start | bytes 1253384 | tf_op jit(solution)/shard_map/ppermute | solution.py:64
  11.1 8.8 %collective-permute-start.3 = (bf16[272,768]{1,0:T(8,128)(2,1)S(1)}, bf16[272,768]{1,0:T(8,128)(2,1)S(1)}, u32[]{:S(2)}, u32[]{:S(2)}) collective-permute-start(bf16[272,768]{1,0:T(8,128)(2,1)S(1)} %get-tuple-element.37), channel_id=1, source_target_pairs={{0,32},{1,192},{2,34},{3,194},{4,36},{5,196},{6,38},{7,198},{8,40}... | collective-permute-start | bytes 1253384 | tf_op jit(solution)/shard_map/ppermute | solution.py:64
  19.9 0.0 collective-permute-done.refs_0_
  20.0 2.4 %collective-permute-start.4 = (bf16[256,768]{1,0:T(8,128)(2,1)S(1)}, bf16[256,768]{1,0:T(8,128)(2,1)S(1)}, u32[]{:S(2)}, u32[]{:S(2)}) collective-permute-start(bf16[256,768]{1,0:T(8,128)(2,1)S(1)} %slice.112), channel_id=1, source_target_pairs={{0,16},{1,17},{2,18},{3,19},{4,20},{5,21},{6,22},{7,23},{8,24},{9,... | collective-permute-start | bytes 1179656 | tf_op jit(solution)/shard_map/ppermute | solution.py:64
  22.4 0.0 collective-permute-done.1.refs_1_
  22.5 3.4 %collective-permute-start.5 = (bf16[256,768]{1,0:T(8,128)(2,1)S(1)}, bf16[256,768]{1,0:T(8,128)(2,1)S(1)}, u32[]{:S(2)}, u32[]{:S(2)}) collective-permute-start(bf16[256,768]{1,0:T(8,128)(2,1)S(1)} %slice.113), channel_id=1, source_target_pairs={{0,16},{1,17},{2,18},{3,19},{4,20},{5,21},{6,22},{7,23},{8,24},{9,... | collective-permute-start | bytes 1179656 | tf_op jit(solution)/shard_map/ppermute | solution.py:64
  25.9 8.9 %collective-permute-done.2.refs_2_ = bf16[272,768]{1,0:T(8,128)(2,1)S(1)} collective-permute-done((bf16[272,768]{1,0:T(8,128)(2,1)S(1)}, bf16[272,768]{1,0:T(8,128)(2,1)S(1)}, u32[]{:S(2)}, u32[]{:S(2)}) %collective-permute-start.2) | collective-permute-done | bytes 417824 | tf_op jit(solution)/shard_map/ppermute | solution.py:64
  34.8 2.4 %collective-permute-start.6 = (bf16[256,768]{1,0:T(8,128)(2,1)S(1)}, bf16[256,768]{1,0:T(8,128)(2,1)S(1)}, u32[]{:S(2)}, u32[]{:S(2)}) collective-permute-start(bf16[256,768]{1,0:T(8,128)(2,1)S(1)} %slice.114), channel_id=1, source_target_pairs={{0,16},{1,17},{2,18},{3,19},{4,20},{5,21},{6,22},{7,23},{8,24},{9,... | collective-permute-start | bytes 1179656 | tf_op jit(solution)/shard_map/ppermute | solution.py:64
  37.3 2.0 %collective-permute-done.3.refs_3_ = bf16[272,768]{1,0:T(8,128)(2,1)S(1)} collective-permute-done((bf16[272,768]{1,0:T(8,128)(2,1)S(1)}, bf16[272,768]{1,0:T(8,128)(2,1)S(1)}, u32[]{:S(2)}, u32[]{:S(2)}) %collective-permute-start.3) | collective-permute-done | bytes 417824 | tf_op jit(solution)/shard_map/ppermute | solution.py:64
  39.3 0.0 copy-start
  39.3 2.5 %collective-permute-start.7 = (bf16[256,768]{1,0:T(8,128)(2,1)S(1)}, bf16[256,768]{1,0:T(8,128)(2,1)S(1)}, u32[]{:S(2)}, u32[]{:S(2)}) collective-permute-start(bf16[256,768]{1,0:T(8,128)(2,1)S(1)} %slice.115), channel_id=1, source_target_pairs={{0,16},{1,17},{2,18},{3,19},{4,20},{5,21},{6,22},{7,23},{8,24},{9,... | collective-permute-start | bytes 1179656 | tf_op jit(solution)/shard_map/ppermute | solution.py:64
  41.8 1.3 pad_maximum_fusion
  43.1 0.0 collective-permute-done.4.refs_4_
  43.1 0.0 collective-permute-done.5.refs_5_
  43.1 5.3 %collective-permute-done.6.refs_6_ = bf16[256,768]{1,0:T(8,128)(2,1)S(1)} collective-permute-done((bf16[256,768]{1,0:T(8,128)(2,1)S(1)}, bf16[256,768]{1,0:T(8,128)(2,1)S(1)}, u32[]{:S(2)}, u32[]{:S(2)}) %collective-permute-start.6) | collective-permute-done | bytes 393248 | tf_op jit(solution)/shard_map/ppermute | solution.py:64
  48.3 8.4 %collective-permute-done.7.refs_7_ = bf16[256,768]{1,0:T(8,128)(2,1)S(1)} collective-permute-done((bf16[256,768]{1,0:T(8,128)(2,1)S(1)}, bf16[256,768]{1,0:T(8,128)(2,1)S(1)}, u32[]{:S(2)}, u32[]{:S(2)}) %collective-permute-start.7) | collective-permute-done | bytes 393248 | tf_op jit(solution)/shard_map/ppermute | solution.py:64
  56.8 1.3 pad_maximum_fusion.1
  58.1 4.1 %collective-permute-start.9 = (bf16[1024,768]{1,0:T(8,128)(2,1)}, bf16[1024,768]{1,0:T(8,128)(2,1)}, u32[]{:S(2)}, u32[]{:S(2)}) collective-permute-start(bf16[1024,768]{1,0:T(8,128)(2,1)} %pad_maximum_fusion.1), channel_id=1, source_target_pairs={{0,1},{1,0},{2,3},{3,2},{4,5},{5,4},{6,7},{7,6},{8,9},{9,8},{10,11... | collective-permute-start | bytes 4718600 | tf_op jit(solution)/shard_map/ppermute | solution.py:64
  62.2 1.9 %collective-permute-start.8 = (bf16[1024,768]{1,0:T(8,128)(2,1)}, bf16[1024,768]{1,0:T(8,128)(2,1)}, u32[]{:S(2)}, u32[]{:S(2)}) collective-permute-start(bf16[1024,768]{1,0:T(8,128)(2,1)} %pad_maximum_fusion), channel_id=1, source_target_pairs={{0,1},{1,0},{2,3},{3,2},{4,5},{5,4},{6,7},{7,6},{8,9},{9,8},{10,11... | collective-permute-start | bytes 4718600 | tf_op jit(solution)/shard_map/ppermute | solution.py:64
  64.2 0.1 pad_add_fusion.blocks_ref
  64.3 0.0 copy-done
  64.3 6.6 %early.1 = (f32[4,8,256]{2,1,0:T(8,128)S(1)}, bf16[2048,768]{1,0:T(8,128)(2,1)S(1)}) custom-call(s32[4]{0:T(128)S(1)} %copy-done, s32[4]{0:T(128)S(1)} %pad_add_fusion.blocks_ref, bf16[272,768]{1,0:T(8,128)(2,1)S(1)} %collective-permute-done.refs_0_, bf16[272,768]{1,0:T(8,128)(2,1)S(1)} %collective-permute-done.1.refs_1_, ...), custom_call_target="tpu_custom_call" | custom-call | flops 3000000000 | bytes 7340032 | tf_op jit(solution)/shard_map/early/pallas_call | solution.py:390
  70.9 0.0 collective-permute-done.9.far_ref
  70.9 0.0 collective-permute-done.8.core_ref
  70.9 35.8 %stats.1 = (f32[4,8,256]{2,1,0:T(8,128)S(1)}, f32[4,256]{1,0:T(4,128)S(1)}, bf16[4096,768]{1,0:T(8,128)(2,1)S(1)}) custom-call(s32[4]{0:T(128)S(1)} %copy-done, s32[4]{0:T(128)S(1)} %pad_add_fusion.blocks_ref, f32[4,8,256]{2,1,0:T(8,128)S(1)} %get-tuple-element.14.part_ref, bf16[2048,768]{1,0:T(8,128)(2,1)S(1)} %get-tuple-element.15.half_ref, ...), custom_call_target="tpu_custom_call" | custom-call | flops 3000000000 | bytes 7340032 | tf_op jit(solution)/shard_map/stats/pallas_call | solution.py:406
  106.7 1.9 %collective-permute-start.10 = (f32[4,8,256]{2,1,0:T(8,128)S(1)}, f32[4,8,256]{2,1,0:T(8,128)S(1)}, u32[]{:S(2)}, u32[]{:S(2)}) collective-permute-start(f32[4,8,256]{2,1,0:T(8,128)S(1)} %get-tuple-element.17), channel_id=1, source_target_pairs={{0,16},{1,17},{2,18},{3,19},{4,20},{5,21},{6,22},{7,23},{8,24},{9,... | collective-permute-start | bytes 98312 | tf_op jit(solution)/shard_map/ppermute | solution.py:64
  108.7 3.8 %collective-permute-done.10 = f32[4,8,256]{2,1,0:T(8,128)S(1)} collective-permute-done((f32[4,8,256]{2,1,0:T(8,128)S(1)}, f32[4,8,256]{2,1,0:T(8,128)S(1)}, u32[]{:S(2)}, u32[]{:S(2)}) %collective-permute-start.10) | collective-permute-done | bytes 32800 | tf_op jit(solution)/shard_map/ppermute | solution.py:64
  112.5 1.9 %collective-permute-start.11 = (f32[2,4,8,256]{3,2,1,0:T(8,128)S(1)}, f32[2,4,8,256]{3,2,1,0:T(8,128)S(1)}, u32[]{:S(2)}, u32[]{:S(2)}) collective-permute-start(f32[2,4,8,256]{3,2,1,0:T(8,128)S(1)} %pad_maximum_fusion.11), channel_id=1, source_target_pairs={{0,1},{1,0},{2,3},{3,2},{4,5},{5,4},{6,7},{7,6},{8,9},{9,8},{10,11... | collective-permute-start | bytes 196616 | tf_op jit(solution)/shard_map/ppermute | solution.py:64
  114.5 1.2 collective-permute-done.11
  115.7 1.7 collective-permute-start.12
  117.4 8.3 %grad.4 = bf16[256,256]{1,0:T(8,128)(2,1)S(1)} custom-call(s32[4]{0:T(128)S(1)} %copy-done, s32[4]{0:T(128)S(1)} %pad_add_fusion.blocks_ref, f32[16,8,256]{2,1,0:T(8,128)S(1)} %fusion.25.stats_ref, bf16[4096,768]{1,0:T(8,128)(2,1)S(1)} %get-tuple-element.18.keys_ref), custom_call_target="tpu_custom_call" | custom-call | flops 2000000000 | bytes 7340032 | tf_op jit(solution)/shard_map/grad/pallas_call | solution.py:423
  125.7 0.0 collective-permute-done.12
  125.7 3.0 %collective-permute-start.13 = (f32[4,256]{1,0:T(4,128)S(1)}, f32[4,256]{1,0:T(4,128)S(1)}, u32[]{:S(2)}, u32[]{:S(2)}) collective-permute-start(f32[4,256]{1,0:T(4,128)S(1)} %add.226), channel_id=1, source_target_pairs={{0,4},{1,5},{2,6},{3,7},{4,0},{5,1},{6,2},{7,3},{8,12},{9,13},{10,... | collective-permute-start | bytes 12296 | tf_op jit(solution)/shard_map/ppermute | solution.py:64
  128.7 7.9 %grad.5 = bf16[256,256]{1,0:T(8,128)(2,1)S(1)} custom-call(s32[4]{0:T(128)S(1)} %copy-done, s32[4]{0:T(128)S(1)} %pad_add_fusion.blocks_ref, f32[16,8,256]{2,1,0:T(8,128)S(1)} %fusion.25.stats_ref, bf16[4096,768]{1,0:T(8,128)(2,1)S(1)} %get-tuple-element.18.keys_ref), custom_call_target="tpu_custom_call" | custom-call | flops 2000000000 | bytes 7340032 | tf_op jit(solution)/shard_map/grad/pallas_call | solution.py:423
  136.6 0.0 collective-permute-done.13
  136.7 2.2 %collective-permute-start.14 = (f32[4,256]{1,0:T(4,128)S(1)}, f32[4,256]{1,0:T(4,128)S(1)}, u32[]{:S(2)}, u32[]{:S(2)}) collective-permute-start(f32[4,256]{1,0:T(4,128)S(1)} %add.227), channel_id=1, source_target_pairs={{0,8},{1,9},{2,10},{3,11},{4,12},{5,13},{6,14},{7,15},{8,0},{9,1},... | collective-permute-start | bytes 12296 | tf_op jit(solution)/shard_map/ppermute | solution.py:64
  138.9 7.8 %grad.6 = bf16[256,256]{1,0:T(8,128)(2,1)S(1)} custom-call(s32[4]{0:T(128)S(1)} %copy-done, s32[4]{0:T(128)S(1)} %pad_add_fusion.blocks_ref, f32[16,8,256]{2,1,0:T(8,128)S(1)} %fusion.25.stats_ref, bf16[4096,768]{1,0:T(8,128)(2,1)S(1)} %get-tuple-element.18.keys_ref), custom_call_target="tpu_custom_call" | custom-call | flops 2000000000 | bytes 7340032 | tf_op jit(solution)/shard_map/grad/pallas_call | solution.py:423
  146.6 0.0 collective-permute-done.14
  146.7 0.7 collective-permute-start.15
  147.4 6.1 %collective-permute-start.16 = (bf16[272,256]{1,0:T(8,128)(2,1)S(1)}, bf16[272,256]{1,0:T(8,128)(2,1)S(1)}, u32[]{:S(2)}, u32[]{:S(2)}) collective-permute-start(bf16[272,256]{1,0:T(8,128)(2,1)S(1)} %pad_maximum_fusion.8), channel_id=1, source_target_pairs={{0,64},{192,65},{2,66},{194,67},{4,68},{196,69},{6,70},{198,71},{8... | collective-permute-start | bytes 417800 | tf_op jit(solution)/shard_map/ppermute | solution.py:64
  153.6 7.1 %collective-permute-start.17 = (bf16[272,256]{1,0:T(8,128)(2,1)S(1)}, bf16[272,256]{1,0:T(8,128)(2,1)S(1)}, u32[]{:S(2)}, u32[]{:S(2)}) collective-permute-start(bf16[272,256]{1,0:T(8,128)(2,1)S(1)} %pad_maximum_fusion.9), channel_id=1, source_target_pairs={{64,0},{128,1},{66,2},{130,3},{68,4},{132,5},{70,6},{134,7},{72,8}... | collective-permute-start | bytes 417800 | tf_op jit(solution)/shard_map/ppermute | solution.py:64
  160.7 8.3 %grad.7 = bf16[256,256]{1,0:T(8,128)(2,1)S(1)} custom-call(s32[4]{0:T(128)S(1)} %copy-done, s32[4]{0:T(128)S(1)} %pad_add_fusion.blocks_ref, f32[16,8,256]{2,1,0:T(8,128)S(1)} %fusion.25.stats_ref, bf16[4096,768]{1,0:T(8,128)(2,1)S(1)} %get-tuple-element.18.keys_ref), custom_call_target="tpu_custom_call" | custom-call | flops 2000000000 | bytes 7340032 | tf_op jit(solution)/shard_map/grad/pallas_call | solution.py:423
  169.1 1.9 %collective-permute-start.18 = (bf16[272,256]{1,0:T(8,128)(2,1)S(1)}, bf16[272,256]{1,0:T(8,128)(2,1)S(1)}, u32[]{:S(2)}, u32[]{:S(2)}) collective-permute-start(bf16[272,256]{1,0:T(8,128)(2,1)S(1)} %pad_maximum_fusion.10), channel_id=1, source_target_pairs={{32,0},{192,1},{34,2},{194,3},{36,4},{196,5},{38,6},{198,7},{40,8}... | collective-permute-start | bytes 417800 | tf_op jit(solution)/shard_map/ppermute | solution.py:64
  171.0 0.0 collective-permute-done.15
  171.0 0.0 collective-permute-done.16
  171.0 0.0 collective-permute-done.17
  171.0 5.0 %collective-permute-done.18 = bf16[272,256]{1,0:T(8,128)(2,1)S(1)} collective-permute-done((bf16[272,256]{1,0:T(8,128)(2,1)S(1)}, bf16[272,256]{1,0:T(8,128)(2,1)S(1)}, u32[]{:S(2)}, u32[]{:S(2)}) %collective-permute-start.18) | collective-permute-done | bytes 139296 | tf_op jit(solution)/shard_map/ppermute | solution.py:64
  176.0 0.1 collective-permute-start.19
  176.2 0.1 pad_maximum_fusion.6
  176.3 0.9 maximum_convert_fusion
  177.3 0.0 collective-permute-done.19
  177.3 0.6 add.236
  (45 shorter events, 0.5 us)
Async XLA Ops:
  0.6 2.5 %copy-start.1 = (f32[256]{0:T(256)S(1)}, f32[256]{0:T(256)}, u32[]{:S(2)}) copy-start(f32[256]{0:T(256)} %param.6) | copy-start | bytes 3076
  3.3 16.6 %collective-permute-start = (bf16[272,768]{1,0:T(8,128)(2,1)S(1)}, bf16[272,768]{1,0:T(8,128)(2,1)S(1)}, u32[]{:S(2)}, u32[]{:S(2)}) collective-permute-start(bf16[272,768]{1,0:T(8,128)(2,1)S(1)} %get-tuple-element.40), channel_id=1, source_target_pairs={{0,0},{1,160},{2,2},{3,162},{4,4},{5,164},{6,6},{7,166},{8,8},{9,1... | collective-permute-start | bytes 1253384 | tf_op jit(solution)/shard_map/ppermute | solution.py:64
  4.0 18.4 %collective-permute-start.1 = (bf16[272,768]{1,0:T(8,128)(2,1)S(1)}, bf16[272,768]{1,0:T(8,128)(2,1)S(1)}, u32[]{:S(2)}, u32[]{:S(2)}) collective-permute-start(bf16[272,768]{1,0:T(8,128)(2,1)S(1)} %get-tuple-element.38), channel_id=1, source_target_pairs={{64,0},{65,192},{66,2},{67,194},{68,4},{69,196},{70,6},{71,198},{7... | collective-permute-start | bytes 1253384 | tf_op jit(solution)/shard_map/ppermute | solution.py:64
  5.3 29.5 %collective-permute-start.2 = (bf16[272,768]{1,0:T(8,128)(2,1)S(1)}, bf16[272,768]{1,0:T(8,128)(2,1)S(1)}, u32[]{:S(2)}, u32[]{:S(2)}) collective-permute-start(bf16[272,768]{1,0:T(8,128)(2,1)S(1)} %get-tuple-element.39), channel_id=1, source_target_pairs={{0,64},{1,128},{2,66},{3,130},{4,68},{5,132},{6,70},{7,134},{8,72}... | collective-permute-start | bytes 1253384 | tf_op jit(solution)/shard_map/ppermute | solution.py:64
  11.1 28.1 %collective-permute-start.3 = (bf16[272,768]{1,0:T(8,128)(2,1)S(1)}, bf16[272,768]{1,0:T(8,128)(2,1)S(1)}, u32[]{:S(2)}, u32[]{:S(2)}) collective-permute-start(bf16[272,768]{1,0:T(8,128)(2,1)S(1)} %get-tuple-element.37), channel_id=1, source_target_pairs={{0,32},{1,192},{2,34},{3,194},{4,36},{5,196},{6,38},{7,198},{8,40}... | collective-permute-start | bytes 1253384 | tf_op jit(solution)/shard_map/ppermute | solution.py:64
  20.0 23.1 %collective-permute-start.4 = (bf16[256,768]{1,0:T(8,128)(2,1)S(1)}, bf16[256,768]{1,0:T(8,128)(2,1)S(1)}, u32[]{:S(2)}, u32[]{:S(2)}) collective-permute-start(bf16[256,768]{1,0:T(8,128)(2,1)S(1)} %slice.112), channel_id=1, source_target_pairs={{0,16},{1,17},{2,18},{3,19},{4,20},{5,21},{6,22},{7,23},{8,24},{9,... | collective-permute-start | bytes 1179656 | tf_op jit(solution)/shard_map/ppermute | solution.py:64
  22.5 20.6 %collective-permute-start.5 = (bf16[256,768]{1,0:T(8,128)(2,1)S(1)}, bf16[256,768]{1,0:T(8,128)(2,1)S(1)}, u32[]{:S(2)}, u32[]{:S(2)}) collective-permute-start(bf16[256,768]{1,0:T(8,128)(2,1)S(1)} %slice.113), channel_id=1, source_target_pairs={{0,16},{1,17},{2,18},{3,19},{4,20},{5,21},{6,22},{7,23},{8,24},{9,... | collective-permute-start | bytes 1179656 | tf_op jit(solution)/shard_map/ppermute | solution.py:64
  34.8 13.5 %collective-permute-start.6 = (bf16[256,768]{1,0:T(8,128)(2,1)S(1)}, bf16[256,768]{1,0:T(8,128)(2,1)S(1)}, u32[]{:S(2)}, u32[]{:S(2)}) collective-permute-start(bf16[256,768]{1,0:T(8,128)(2,1)S(1)} %slice.114), channel_id=1, source_target_pairs={{0,16},{1,17},{2,18},{3,19},{4,20},{5,21},{6,22},{7,23},{8,24},{9,... | collective-permute-start | bytes 1179656 | tf_op jit(solution)/shard_map/ppermute | solution.py:64
  39.3 25.0 %copy-start = (s32[4]{0:T(128)S(1)}, s32[4]{0:T(128)}, u32[]{:S(2)}) copy-start(s32[4]{0:T(128)} %lengths_ref.11) | copy-start | bytes 52
  39.3 17.5 %collective-permute-start.7 = (bf16[256,768]{1,0:T(8,128)(2,1)S(1)}, bf16[256,768]{1,0:T(8,128)(2,1)S(1)}, u32[]{:S(2)}, u32[]{:S(2)}) collective-permute-start(bf16[256,768]{1,0:T(8,128)(2,1)S(1)} %slice.115), channel_id=1, source_target_pairs={{0,16},{1,17},{2,18},{3,19},{4,20},{5,21},{6,22},{7,23},{8,24},{9,... | collective-permute-start | bytes 1179656 | tf_op jit(solution)/shard_map/ppermute | solution.py:64
  58.1 12.8 %collective-permute-start.9 = (bf16[1024,768]{1,0:T(8,128)(2,1)}, bf16[1024,768]{1,0:T(8,128)(2,1)}, u32[]{:S(2)}, u32[]{:S(2)}) collective-permute-start(bf16[1024,768]{1,0:T(8,128)(2,1)} %pad_maximum_fusion.1), channel_id=1, source_target_pairs={{0,1},{1,0},{2,3},{3,2},{4,5},{5,4},{6,7},{7,6},{8,9},{9,8},{10,11... | collective-permute-start | bytes 4718600 | tf_op jit(solution)/shard_map/ppermute | solution.py:64
  62.2 8.7 %collective-permute-start.8 = (bf16[1024,768]{1,0:T(8,128)(2,1)}, bf16[1024,768]{1,0:T(8,128)(2,1)}, u32[]{:S(2)}, u32[]{:S(2)}) collective-permute-start(bf16[1024,768]{1,0:T(8,128)(2,1)} %pad_maximum_fusion), channel_id=1, source_target_pairs={{0,1},{1,0},{2,3},{3,2},{4,5},{5,4},{6,7},{7,6},{8,9},{9,8},{10,11... | collective-permute-start | bytes 4718600 | tf_op jit(solution)/shard_map/ppermute | solution.py:64
  106.7 5.8 %collective-permute-start.10 = (f32[4,8,256]{2,1,0:T(8,128)S(1)}, f32[4,8,256]{2,1,0:T(8,128)S(1)}, u32[]{:S(2)}, u32[]{:S(2)}) collective-permute-start(f32[4,8,256]{2,1,0:T(8,128)S(1)} %get-tuple-element.17), channel_id=1, source_target_pairs={{0,16},{1,17},{2,18},{3,19},{4,20},{5,21},{6,22},{7,23},{8,24},{9,... | collective-permute-start | bytes 98312 | tf_op jit(solution)/shard_map/ppermute | solution.py:64
  112.5 3.1 %collective-permute-start.11 = (f32[2,4,8,256]{3,2,1,0:T(8,128)S(1)}, f32[2,4,8,256]{3,2,1,0:T(8,128)S(1)}, u32[]{:S(2)}, u32[]{:S(2)}) collective-permute-start(f32[2,4,8,256]{3,2,1,0:T(8,128)S(1)} %pad_maximum_fusion.11), channel_id=1, source_target_pairs={{0,1},{1,0},{2,3},{3,2},{4,5},{5,4},{6,7},{7,6},{8,9},{9,8},{10,11... | collective-permute-start | bytes 196616 | tf_op jit(solution)/shard_map/ppermute | solution.py:64
  115.7 10.0 %collective-permute-start.12 = (f32[4,256]{1,0:T(4,128)S(1)}, f32[4,256]{1,0:T(4,128)S(1)}, u32[]{:S(2)}, u32[]{:S(2)}) collective-permute-start(f32[4,256]{1,0:T(4,128)S(1)} %get-tuple-element.20), channel_id=1, source_target_pairs={{0,2},{1,3},{2,0},{3,1},{4,6},{5,7},{6,4},{7,5},{8,10},{9,11},{10,... | collective-permute-start | bytes 12296 | tf_op jit(solution)/shard_map/ppermute | solution.py:64
  125.7 10.9 %collective-permute-start.13 = (f32[4,256]{1,0:T(4,128)S(1)}, f32[4,256]{1,0:T(4,128)S(1)}, u32[]{:S(2)}, u32[]{:S(2)}) collective-permute-start(f32[4,256]{1,0:T(4,128)S(1)} %add.226), channel_id=1, source_target_pairs={{0,4},{1,5},{2,6},{3,7},{4,0},{5,1},{6,2},{7,3},{8,12},{9,13},{10,... | collective-permute-start | bytes 12296 | tf_op jit(solution)/shard_map/ppermute | solution.py:64
  136.7 10.0 %collective-permute-start.14 = (f32[4,256]{1,0:T(4,128)S(1)}, f32[4,256]{1,0:T(4,128)S(1)}, u32[]{:S(2)}, u32[]{:S(2)}) collective-permute-start(f32[4,256]{1,0:T(4,128)S(1)} %add.227), channel_id=1, source_target_pairs={{0,8},{1,9},{2,10},{3,11},{4,12},{5,13},{6,14},{7,15},{8,0},{9,1},... | collective-permute-start | bytes 12296 | tf_op jit(solution)/shard_map/ppermute | solution.py:64
  146.7 24.3 %collective-permute-start.15 = (bf16[272,256]{1,0:T(8,128)(2,1)S(1)}, bf16[272,256]{1,0:T(8,128)(2,1)S(1)}, u32[]{:S(2)}, u32[]{:S(2)}) collective-permute-start(bf16[272,256]{1,0:T(8,128)(2,1)S(1)} %pad_maximum_fusion.7), channel_id=1, source_target_pairs={{0,0},{160,1},{2,2},{162,3},{4,4},{164,5},{6,6},{166,7},{8,8},{168... | collective-permute-start | bytes 417800 | tf_op jit(solution)/shard_map/ppermute | solution.py:64
  147.4 23.6 %collective-permute-start.16 = (bf16[272,256]{1,0:T(8,128)(2,1)S(1)}, bf16[272,256]{1,0:T(8,128)(2,1)S(1)}, u32[]{:S(2)}, u32[]{:S(2)}) collective-permute-start(bf16[272,256]{1,0:T(8,128)(2,1)S(1)} %pad_maximum_fusion.8), channel_id=1, source_target_pairs={{0,64},{192,65},{2,66},{194,67},{4,68},{196,69},{6,70},{198,71},{8... | collective-permute-start | bytes 417800 | tf_op jit(solution)/shard_map/ppermute | solution.py:64
  153.6 17.4 %collective-permute-start.17 = (bf16[272,256]{1,0:T(8,128)(2,1)S(1)}, bf16[272,256]{1,0:T(8,128)(2,1)S(1)}, u32[]{:S(2)}, u32[]{:S(2)}) collective-permute-start(bf16[272,256]{1,0:T(8,128)(2,1)S(1)} %pad_maximum_fusion.9), channel_id=1, source_target_pairs={{64,0},{128,1},{66,2},{130,3},{68,4},{132,5},{70,6},{134,7},{72,8}... | collective-permute-start | bytes 417800 | tf_op jit(solution)/shard_map/ppermute | solution.py:64
  169.1 6.9 %collective-permute-start.18 = (bf16[272,256]{1,0:T(8,128)(2,1)S(1)}, bf16[272,256]{1,0:T(8,128)(2,1)S(1)}, u32[]{:S(2)}, u32[]{:S(2)}) collective-permute-start(bf16[272,256]{1,0:T(8,128)(2,1)S(1)} %pad_maximum_fusion.10), channel_id=1, source_target_pairs={{32,0},{192,1},{34,2},{194,3},{36,4},{196,5},{38,6},{198,7},{40,8}... | collective-permute-start | bytes 417800 | tf_op jit(solution)/shard_map/ppermute | solution.py:64
  176.0 1.2 collective-permute-start.19
